TPU v7x, 32 devices: a whole 2x2x4 slice. The times are simulated.
32 devices in a mesh: section: 4 (over y, x), tensor: 4 (over z), dp: 2 (over core).
Axes of the slice: x: 2, y: 2, z: 4, core: 2. Of those that a mesh axis runs over, the one named last changes fastest.
Arguments:
- fwd_in: bfloat16 [4, 128, 4096], P('section', 'dp', 'tensor'), may hold values from -6 to 6
- back_in: bfloat16 [4, 128, 4096], P('section', 'dp', 'tensor'), may hold values from -6 to 6
- back_grad: bfloat16 [4, 128, 4096], P('section', 'dp', 'tensor'), may hold values from -6 to 6
- gain: float32 [4, 4096], P('section'), may hold values from 0.25 to 1.75
- w_query: bfloat16 [4, 4096, 4096], P('section', 'dp', 'tensor'), may hold values from -0.09375 to 0.09375
- w_out: bfloat16 [4, 4096, 4096], P('section', 'dp', 'tensor'), may hold values from -0.75 to 0.75
- neighbour_kv: bfloat16 [4, 1024, 2, 4096], P(None, ('section', 'tensor', 'dp')), may hold values from -6 to 6
- pattern: int32 [2, 2, 2], P(None, 'dp'), may hold values from 0 to 3
Outputs:
- next_in: bfloat16 [4, 128, 4096], P('section', 'dp', 'tensor')
- prev_grad: bfloat16 [4, 128, 4096], P('section', 'dp', 'tensor')
- kv_grad: bfloat16 [4, 1024, 2, 4096], P(None, ('section', 'tensor', 'dp'))
- gain_grad: float32 [4, 4096], P('section', 'tensor')
Inputs may be any that keep to these rules, and one draw needn't show every extreme that they name: `pattern`: each entry numbers one of the 4 neighbour blocks of the span's own group.
All inputs are finite; a program needn't handle non-finite values.
Results may differ from a plain program's by a relative error of at most 0.012.
Values may be sent and summed in bfloat16 or wider, within the bound.
A program may use at most 64 MiB of HBM per device.

v0:
```python
import jax
import jax.numpy as jnp
from jax import lax
from jax.sharding import PartitionSpec as P

D = 4096
HD = 128
SPAN = 64
NBR = 2
NBR_LEN = 128
CPM = 1
NBLK_DP = 4


norm_eps = 1e-05


def passed_along(array, axis, by):
    devices = lax.axis_size(axis)
    return lax.ppermute(array, axis, [(i, (i + by) % devices) for i in range(devices)])


def shifted(value, axis, steps):
    count = lax.axis_size(axis)
    leading, last = (max(0, -steps), min(count, count - steps))
    return lax.ppermute(value, axis, [(source, source + steps) for source in range(leading, last)])


def attend(queries, key_rows, values):
    score_scale = queries.shape[-1] ** (-0.5)
    scores = (
        jnp.einsum("clhe,crhe->chlr", queries, key_rows, preferred_element_type=jnp.float32)
        * score_scale
    )
    soft_probs = jax.nn.softmax(scores, axis=-1)
    blended = jnp.einsum(
        "chlr,crhe->clhe",
        soft_probs.astype(jnp.bfloat16),
        values,
        preferred_element_type=jnp.float32,
    )
    return (blended.astype(jnp.bfloat16), soft_probs)


def attend_back(grad_out, soft_probs, queries, key_rows, values):
    score_scale = queries.shape[-1] ** (-0.5)
    rounded = soft_probs.astype(jnp.bfloat16)
    grad_values = jnp.einsum(
        "chlr,clhe->crhe", rounded, grad_out, preferred_element_type=jnp.float32
    )
    grad_probs = jnp.einsum("clhe,crhe->chlr", grad_out, values, preferred_element_type=jnp.float32)
    grad_scores = soft_probs * (
        grad_probs - jnp.sum(grad_probs * soft_probs, axis=-1, keepdims=True)
    )
    scaled = (grad_scores * score_scale).astype(jnp.bfloat16)
    grad_queries = jnp.einsum(
        "chlr,crhe->clhe", scaled, key_rows, preferred_element_type=jnp.float32
    ).astype(jnp.bfloat16)
    grad_keys = jnp.einsum("chlr,clhe->crhe", scaled, queries, preferred_element_type=jnp.float32)
    return (grad_queries, grad_keys, grad_values)


def on_device(fwd_in, back_in, back_grad, gain, w_query, w_out, neighbour_kv, pattern):
    sections = lax.axis_size("section")
    tensor_count = lax.axis_size("tensor")
    width_cols = fwd_in.shape[2]
    token_count = fwd_in.shape[1]
    col_start = lax.axis_index("tensor") * width_cols
    gain_full = gain[0]
    gain_cols = lax.dynamic_slice_in_dim(gain_full, col_start, width_cols)
    kv_local = lax.all_to_all(
        lax.all_to_all(neighbour_kv, "section", split_axis=0, concat_axis=1, tiled=True),
        "tensor",
        split_axis=3,
        concat_axis=1,
        tiled=True,
    )
    heads_dev = kv_local.shape[3] // HD
    inner_dev = heads_dev * HD
    blocks = kv_local[0].reshape(NBLK_DP, NBR_LEN, 2, heads_dev, HD)
    query_full, out_full = (
        lax.all_gather(w_query, "dp", axis=1, tiled=True),
        lax.all_gather(w_out, "dp", axis=1, tiled=True),
    )
    query_slab = query_full[0]
    out_slab = out_full[0]
    span_picks = pattern.reshape(2 * CPM, NBR)
    picked = blocks[span_picks]
    key_rows = picked[:, :, :, 0].reshape(2 * CPM, NBR * NBR_LEN, heads_dev, HD)
    values = picked[:, :, :, 1].reshape(2 * CPM, NBR * NBR_LEN, heads_dev, HD)
    both_rows = jnp.concatenate([fwd_in[0], back_in[0]], axis=0)
    wide_rows = lax.all_gather(both_rows, "tensor", axis=1, tiled=True).astype(jnp.float32)
    inv_rms = lax.rsqrt(jnp.mean(wide_rows * wide_rows, axis=-1) + norm_eps)
    normed = (wide_rows * inv_rms[:, None] * gain_full).astype(jnp.bfloat16)
    queries = jnp.dot(normed, query_slab, preferred_element_type=jnp.float32).astype(jnp.bfloat16)
    queries = queries.reshape(2 * CPM, SPAN, heads_dev, HD)
    blended, soft_probs = attend(queries, key_rows, values)
    forward_blended = blended[:CPM].reshape(token_count, inner_dev)
    projected = jnp.dot(
        lax.all_gather(forward_blended, "tensor", axis=1, tiled=True),
        out_slab,
        preferred_element_type=jnp.float32,
    )
    forward_result = (fwd_in[0].astype(jnp.float32) + projected).astype(jnp.bfloat16)
    next_in = passed_along(forward_result, "section", 1)
    grad_out = back_grad[0]
    out_terms = lax.dot_general(
        grad_out, out_slab, (((1,), (1,)), ((), ())), preferred_element_type=jnp.float32
    )
    grad_blended = lax.psum_scatter(out_terms, "tensor", scatter_dimension=1, tiled=True).astype(
        jnp.bfloat16
    )
    grad_blended = grad_blended.reshape(CPM, SPAN, heads_dev, HD)
    grad_queries, grad_keys, grad_values = attend_back(
        grad_blended, soft_probs[CPM:], queries[CPM:], key_rows[CPM:], values[CPM:]
    )
    grad_flat = grad_queries.reshape(token_count, inner_dev)
    query_terms = lax.dot_general(
        grad_flat, query_slab, (((1,), (1,)), ((), ())), preferred_element_type=jnp.float32
    )
    grad_normed = lax.psum_scatter(query_terms, "tensor", scatter_dimension=1, tiled=True)
    back_cols = back_in[0].astype(jnp.float32)
    back_rms = inv_rms[token_count:]
    row_total = lax.psum(jnp.sum(grad_normed * gain_cols * back_cols, axis=-1), "tensor")
    grad_wide = grad_out.astype(jnp.float32) + gain_cols * back_rms[:, None] * grad_normed
    grad_wide = grad_wide - back_cols * (back_rms * back_rms * back_rms * row_total / D)[:, None]
    grad_in = grad_wide.astype(jnp.bfloat16)
    prev_grad = shifted(grad_in, "section", -1)
    onehot = (span_picks[CPM:][..., None] == jnp.arange(NBLK_DP, dtype=jnp.int32)).astype(
        jnp.float32
    )
    key_blocks = jnp.einsum(
        "cjb,cjrhe->brhe", onehot, grad_keys.reshape(CPM, NBR, NBR_LEN, heads_dev, HD)
    )
    value_blocks = jnp.einsum(
        "cjb,cjrhe->brhe", onehot, grad_values.reshape(CPM, NBR, NBR_LEN, heads_dev, HD)
    )
    kv_blocks = jnp.stack([key_blocks, value_blocks], axis=2)
    gain_part = jnp.sum(grad_normed * back_cols * back_rms[:, None], axis=0)
    gain_grad = lax.psum(gain_part, "dp")
    shard_rows = NBLK_DP * NBR_LEN // (sections * tensor_count)
    kv_grad = kv_blocks.astype(jnp.bfloat16).reshape(
        tensor_count, sections, shard_rows, 2, inner_dev
    )
    kv_grad = kv_grad.transpose(1, 0, 2, 3, 4).reshape(1, NBLK_DP * NBR_LEN, 2, inner_dev)
    kv_grad = lax.all_to_all(
        lax.all_to_all(kv_grad, "section", split_axis=1, concat_axis=0, tiled=True),
        "tensor",
        split_axis=1,
        concat_axis=3,
        tiled=True,
    )
    return (next_in[None], prev_grad[None], kv_grad, gain_grad[None])


def solution(mesh):
    return jax.shard_map(
        on_device,
        mesh=mesh,
        in_specs=(
            P("section", "dp", "tensor"),
            P("section", "dp", "tensor"),
            P("section", "dp", "tensor"),
            P("section", None),
            P("section", "dp", "tensor"),
            P("section", "dp", "tensor"),
            P(None, ("section", "tensor", "dp"), None, None),
            P(None, "dp", None),
        ),
        out_specs=(
            P("section", "dp", "tensor"),
            P("section", "dp", "tensor"),
            P(None, ("section", "tensor", "dp"), None, None),
            P("section", "tensor"),
        ),
        check_vma=False,
    )
```

profile of v0, /device:TPU:0, one launch (start us, length us, event | category | flops | bytes accessed | tf_op | source)
XLA Modules:
  0.0 296.0 jit_solution(13906292855031881132)
XLA Ops:
  11.8 30.3 %all_to_all.57 = bf16[4,32,2,4096]{3,1,2,0:T(8,128)(2,1)S(1)} all-to-all(bf16[4,32,2,4096]{3,1,2,0:T(8,128)(2,1)S(1)} %copy.178), channel_id=1, replica_groups=mesh['section'=4,'tensor'=4,'dp'=2] {'section'}, dimensions={0} | all-to-all | bytes 4194304 | tf_op jit(solution)/shard_map/all_to_all | solution.py:72
  42.3 3.8 %copy.180 = bf16[1,128,2,4096]{1,2,0,3:T(2,128)(2,1)} copy(bf16[1,128,2,4096]{3,1,2,0:T(8,128)(2,1)S(1)} %bitcast.161) | data formatting | bytes 4194304 | tf_op jit(solution)/shard_map/all_to_all | solution.py:72
  46.0 5.0 %all-to-all-start.1 = ((bf16[1,128,2,4096]{1,2,0,3:T(2,128)(2,1)}), bf16[1,128,2,4096]{1,2,0,3:T(2,128)(2,1)S(1)}, u32[]{:S(2)}, u32[]{:S(2)}) async-start(bf16[1,128,2,4096]{1,2,0,3:T(2,128)(2,1)} %copy.180), calls=%async_computation.1 | async-start | bytes 4194304 | tf_op jit(solution)/shard_map/all_to_all | solution.py:71
  51.2 7.1 %fusion.1 = f32[64,4096]{1,0:T(8,128)} fusion(bf16[1,4096,1024]{2,1,0:T(8,128)(2,1)} %all-gather.8.cloned.1.call-done, bf16[1,64,1024]{2,1,0:T(8,128)(2,1)S(1)} %copy-done.5), kind=kOutput, calls=%fused_computation.2 | convolution fusion | flops 536870912 | bytes 9568256 | tf_op jit(solution)/shard_map/dot_general | solution.py:107
  58.3 21.1 %all-gather.4.cloned.1.call-done = bf16[128,4096]{1,0:T(8,128)(2,1)} async-done(((bf16[128,1024]{1,0:T(8,128)(2,1)}), bf16[128,4096]{1,0:T(8,128)(2,1)}) %all-gather.4.cloned.1.call-update) | async-done | bytes 1048592 | tf_op jit(solution)/shard_map/all_gather | solution.py:92
  80.9 27.1 %all-to-all-done.1 = bf16[1,128,2,4096]{1,2,0,3:T(2,128)(2,1)S(1)} async-done(((bf16[1,128,2,4096]{1,2,0,3:T(2,128)(2,1)}), bf16[1,128,2,4096]{1,2,0,3:T(2,128)(2,1)S(1)}, u32[]{:S(2)}, u32[]{:S(2)}) %all-to-all-start.1) | async-done | bytes 2097184 | tf_op jit(solution)/shard_map/all_to_all | solution.py:71
  109.6 3.0 %copy.183 = bf16[4,128,2,8,128]{4,1,2,3,0:T(8,128)(2,1)S(1)} copy(bf16[4,128,2,8,128]{1,4,3,0,2:T(8,128)(2,1)} %bitcast.162) | data formatting | bytes 4194304 | tf_op jit(solution)/shard_map/reshape;squeeze | solution.py:80
  112.6 2.1 gather_fusion
  114.8 3.0 copy.184
  120.5 5.1 %fusion.16 = bf16[128,1024]{1,0:T(8,128)(2,1)S(1)} fusion(bf16[1,4096,1024]{2,1,0:T(8,128)(2,1)} %all-gather.6.cloned.1.call-done, bf16[128,4096]{1,0:T(8,128)(2,1)} %all-gather.4.cloned.1.call-done, f32[4096]{0:T(1024)S(1)} %bitcast.183, f32[128]{0:T(128)S(1)} %add_rsqrt_fusion), kind=kOutput, calls=%fused_computation.25 | convolution fusion | flops 1075970048 | bytes 9716224 | tf_op jit(solution)/shard_map/dot_general | solution.py:95
  126.5 3.7 %reduce-scatter.3.cloned.1.call-done = f32[64,1024]{1,0:T(8,128)} async-done(((f32[64,4096]{1,0:T(8,128)}), f32[64,1024]{1,0:T(8,128)}) %reduce-scatter.3.cloned.1.call-update) | async-done | bytes 262160 | tf_op jit(solution)/shard_map/reduce_scatter | solution.py:110
  137.3 2.0 fusion.13
  141.5 3.5 %copy.198 = bf16[1,512,2,1024]{3,2,0,1:T(2,128)(2,1)} copy(bf16[1,512,2,1024]{3,1,2,0:T(8,128)(2,1)S(1)} %bitcast.163) | data formatting | bytes 4194304 | tf_op jit(solution)/shard_map/reshape | solution.py:145
  145.0 3.6 %all-to-all-start.2 = ((bf16[1,512,2,1024]{3,2,0,1:T(2,128)(2,1)}), bf16[1,512,2,1024]{3,2,0,1:T(2,128)(2,1)S(1)}, u32[]{:S(2)}, u32[]{:S(2)}) async-start(bf16[1,512,2,1024]{3,2,0,1:T(2,128)(2,1)} %copy.198), calls=%async_computation.4 | async-start | bytes 4194304 | tf_op jit(solution)/shard_map/all_to_all | solution.py:147
  150.1 23.4 %all-to-all-done.2 = bf16[1,512,2,1024]{3,2,0,1:T(2,128)(2,1)S(1)} async-done(((bf16[1,512,2,1024]{3,2,0,1:T(2,128)(2,1)}), bf16[1,512,2,1024]{3,2,0,1:T(2,128)(2,1)S(1)}, u32[]{:S(2)}, u32[]{:S(2)}) %all-to-all-start.2) | async-done | bytes 2097184 | tf_op jit(solution)/shard_map/all_to_all | solution.py:147
  173.5 3.7 %copy.199 = bf16[4,128,2,1024]{3,2,0,1:T(2,128)(2,1)} copy(bf16[4,128,2,1024]{3,2,1,0:T(2,128)(2,1)S(1)} %bitcast.160) | data formatting | bytes 4194304 | tf_op jit(solution)/shard_map/all_to_all | solution.py:147
  177.2 3.6 %all-to-all-start.3 = ((bf16[4,128,2,1024]{3,2,0,1:T(2,128)(2,1)}), bf16[4,128,2,1024]{3,2,0,1:T(2,128)(2,1)S(1)}, u32[]{:S(2)}, u32[]{:S(2)}) async-start(bf16[4,128,2,1024]{3,2,0,1:T(2,128)(2,1)} %copy.199), calls=%async_computation.5 | async-start | bytes 4194304 | tf_op jit(solution)/shard_map/all_to_all | solution.py:146
  180.9 7.0 %fusion.5 = f32[64,4096]{1,0:T(8,128)} fusion(bf16[1,4096,1024]{2,1,0:T(8,128)(2,1)} %all-gather.6.cloned.1.call-done, bf16[8,8,8,128]{3,2,1,0:T(8,128)(2,1)S(1)} %bitcast.174), kind=kOutput, calls=%fused_computation.6 | convolution fusion | flops 536870912 | bytes 9568256 | tf_op jit(solution)/shard_map/dot_general | solution.py:118
  190.7 65.0 %all_gather.14 = bf16[64,4096]{1,0:T(8,128)(2,1)S(1)} all-gather(bf16[64,1024]{1,0:T(8,128)(2,1)S(1)} %bitcast.176), channel_id=1, replica_groups=mesh['section'=4,'tensor'=4,'dp'=2] {'tensor'}, dimensions={1}, use_global_device_ids=true | all-gather | bytes 655360 | tf_op jit(solution)/shard_map/all_gather | solution.py:100
  255.7 5.0 %fusion.23 = bf16[64,1024]{1,0:T(8,128)(2,1)S(1)} fusion(bf16[64,4096]{1,0:T(8,128)(2,1)S(1)} %all_gather.14, bf16[1,4096,1024]{2,1,0:T(8,128)(2,1)} %all-gather.8.cloned.1.call-done, bf16[1,64,1024]{2,1,0:T(8,128)(2,1)S(1)} %copy-done.8), kind=kOutput, calls=%fused_computation.30 | convolution fusion | flops 537067520 | bytes 9175040 | tf_op jit(solution)/shard_map/dot_general | solution.py:99
  263.0 11.7 %psum.14 = f32[64]{0:T(128)S(1)} all-reduce(f32[64]{0:T(128)S(1)} %get-tuple-element.37), channel_id=1, replica_groups=mesh['section'=4,'tensor'=4,'dp'=2] {'tensor'}, use_global_device_ids=true, to_apply=%region_7.0 | all-reduce | flops 64 | bytes 512 | tf_op jit(solution)/shard_map/psum | solution.py:124
  277.2 3.1 %psum.15 = f32[1,1024]{1,0:T(1,128)} all-reduce(f32[1,1024]{1,0:T(1,128)S(1)} %bitcast.182), channel_id=1, replica_groups=mesh['section'=4,'tensor'=4,'dp'=2] {'dp'}, use_global_device_ids=true, to_apply=%region_9.0 | all-reduce | flops 1024 | bytes 8192 | tf_op jit(solution)/shard_map/psum | solution.py:140
  280.3 2.5 collective-permute-done.1
  285.6 2.6 reshape.242
  (92 shorter events, 33.9 us)
Async XLA Ops:
  7.2 0.9 copy-start.1
  7.2 1.0 copy-start.7
  7.2 44.0 %all-gather.8.cloned.1.call-start = ((), (), s32[]{:S(2)}) async-start(), calls=%async_computation.8 | async-start | bytes 12582912 | tf_op jit(solution)/shard_map/all_gather | solution.py:83
  7.9 71.5 %all-gather.4.cloned.1.call-start = ((), (), s32[]{:S(2)}) async-start(), calls=%async_computation.6 | async-start | bytes 1310720 | tf_op jit(solution)/shard_map/all_gather | solution.py:92
  8.9 1.6 copy-start
  8.9 111.5 %all-gather.6.cloned.1.call-start = ((), (), s32[]{:S(2)}) async-start(), calls=%async_computation.7 | async-start | bytes 12582912 | tf_op jit(solution)/shard_map/all_gather | solution.py:82
  46.0 5.0 %copy-start.13 = (s32[2,1,2]{2,1,0:T(1,128)S(1)}, s32[2,1,2]{2,1,0:T(1,128)}, u32[]{:S(2)}) copy-start(s32[2,1,2]{2,1,0:T(1,128)} %param.15) | copy-start | bytes 52
  46.0 5.1 %copy-start.5 = (bf16[1,64,1024]{2,1,0:T(8,128)(2,1)S(1)}, bf16[1,64,1024]{2,1,0:T(8,128)(2,1)}, u32[]{:S(2)}) copy-start(bf16[1,64,1024]{2,1,0:T(8,128)(2,1)} %param.10) | copy-start | bytes 393220
  46.0 62.0 %all-to-all-start.1 = ((bf16[1,128,2,4096]{1,2,0,3:T(2,128)(2,1)}), bf16[1,128,2,4096]{1,2,0,3:T(2,128)(2,1)S(1)}, u32[]{:S(2)}, u32[]{:S(2)}) async-start(bf16[1,128,2,4096]{1,2,0,3:T(2,128)(2,1)} %copy.180), calls=%async_computation.1 | async-start | bytes 4194304 | tf_op jit(solution)/shard_map/all_to_all | solution.py:71
  51.0 79.1 %reduce-scatter.3.cloned.1.call-start = ((), (), s32[]{:S(2)}) async-start(), calls=%async_computation.9 | async-start | bytes 1310720 | tf_op jit(solution)/shard_map/reduce_scatter | solution.py:110
  119.3 1.1 copy-start.12
  125.5 0.9 copy-start.3
  130.2 2.9 copy-start.2
  133.1 0.9 copy-start.4
  134.0 1.9 copy-start.9
  145.0 28.5 %all-to-all-start.2 = ((bf16[1,512,2,1024]{3,2,0,1:T(2,128)(2,1)}), bf16[1,512,2,1024]{3,2,0,1:T(2,128)(2,1)S(1)}, u32[]{:S(2)}, u32[]{:S(2)}) async-start(bf16[1,512,2,1024]{3,2,0,1:T(2,128)(2,1)} %copy.198), calls=%async_computation.4 | async-start | bytes 4194304 | tf_op jit(solution)/shard_map/all_to_all | solution.py:147
  177.2 105.5 %all-to-all-start.3 = ((bf16[4,128,2,1024]{3,2,0,1:T(2,128)(2,1)}), bf16[4,128,2,1024]{3,2,0,1:T(2,128)(2,1)S(1)}, u32[]{:S(2)}, u32[]{:S(2)}) async-start(bf16[4,128,2,1024]{3,2,0,1:T(2,128)(2,1)} %copy.199), calls=%async_computation.5 | async-start | bytes 4194304 | tf_op jit(solution)/shard_map/all_to_all | solution.py:146
  180.9 81.0 %reduce-scatter.5.cloned.1.call-start = ((), (), s32[]{:S(2)}) async-start(), calls=%async_computation.10 | async-start | bytes 1310720 | tf_op jit(solution)/shard_map/reduce_scatter | solution.py:121
  190.2 65.5 %copy-start.8 = (bf16[1,64,1024]{2,1,0:T(8,128)(2,1)S(1)}, bf16[1,64,1024]{2,1,0:T(8,128)(2,1)}, u32[]{:S(2)}) copy-start(bf16[1,64,1024]{2,1,0:T(8,128)(2,1)} %param.8) | copy-start | bytes 393220
  255.7 19.1 %copy-start.6 = (bf16[1,64,1024]{2,1,0:T(8,128)(2,1)S(1)}, bf16[1,64,1024]{2,1,0:T(8,128)(2,1)}, u32[]{:S(2)}) copy-start(bf16[1,64,1024]{2,1,0:T(8,128)(2,1)} %param.10) | copy-start | bytes 393220
  260.7 16.5 %collective-permute-start = (bf16[64,1024]{1,0:T(8,128)(2,1)S(1)}, bf16[64,1024]{1,0:T(8,128)(2,1)S(1)}, u32[]{:S(2)}, u32[]{:S(2)}) collective-permute-start(bf16[64,1024]{1,0:T(8,128)(2,1)S(1)} %fusion.23), channel_id=1, source_target_pairs={{0,8},{8,16},{16,24},{24,0},{1,9},{9,17},{17,25},{25,1},{2,10},{10... | collective-permute-start | bytes 393224 | tf_op jit(solution)/shard_map/ppermute | solution.py:20
  275.9 6.9 %collective-permute-start.1 = (bf16[64,1024]{1,0:T(8,128)(2,1)S(1)}, bf16[64,1024]{1,0:T(8,128)(2,1)S(1)}, u32[]{:S(2)}, u32[]{:S(2)}) collective-permute-start(bf16[64,1024]{1,0:T(8,128)(2,1)S(1)} %fusion.36), channel_id=1, source_target_pairs={{8,0},{16,8},{24,16},{9,1},{17,9},{25,17},{10,2},{18,10},{26,18},{... | collective-permute-start | bytes 393224 | tf_op jit(solution)/shard_map/ppermute | solution.py:26
  277.2 6.7 %copy-start.10 = (bf16[64,1024]{1,0:T(8,128)(2,1)}, bf16[64,1024]{1,0:T(8,128)(2,1)S(1)}, u32[]{:S(2)}) copy-start(bf16[64,1024]{1,0:T(8,128)(2,1)S(1)} %collective-permute-done) | copy-start | bytes 393220
  285.5 2.6 copy-start.11
Sparse Core Ops, SparseCore 0:
  9.6 22.5 all-gather.7
  33.7 45.6 all-gather.3
  80.9 18.6 all-gather.5
  101.8 28.3 reduce-scatter.2
  188.1 53.5 reduce-scatter.4
where the time goes:
time: 297 us; the launch traced here: 296 us
  blocking collectives  110 us (37%)
  waiting for transfers between devices  79.3 us (27%)
  local copies, waits for them, and re-layouts  40.4 us (14%)
  matrix products  30.8 us (10%)
  starting transfers between devices  14.8 us (5%)
  between operations  14.2 us (5%)
  other arithmetic  6.41 us (2%)
    all_gather x1, blocking collectives, on_device(): lax.all_gather(forward_blended, 'tensor', axis=1, tiled=True)  65 us
    all_to_all x1, blocking collectives, on_device(): lax.all_to_all(neighbour_kv, 'section', split_axis=0, concat_axis=1, tile...  30.3 us
    all_to_all x1, waiting for transfers between devices, on_device(): lax.all_to_all(lax.all_to_all(neighbour_kv, 'section', split_axis=0, conc...  27.1 us
    all_to_all x1, waiting for transfers between devices, on_device(): lax.all_to_all(kv_grad, 'section', split_axis=1, concat_axis=0, tiled=True)  23.4 us
    all_gather x1, waiting for transfers between devices, on_device(): lax.all_gather(both_rows, 'tensor', axis=1, tiled=True).astype(jnp.float32)  21.1 us
    psum x1, blocking collectives, on_device(): lax.psum(jnp.sum(grad_normed * gain_cols * back_cols, axis=-1), 'tensor')  11.7 us
    unnamed x35, local copies, waits for them, and re-layouts  8.42 us
    dot_general x1, matrix products, on_device(): lax.dot_general(grad_out, out_slab, (((1,), (1,)), ((), ())), preferred_e...  7.05 us
  transfers between devices with their start and end apart: 10, of which 5 were waited for; matrix products, arithmetic and copies ran while one was open for 17% of the time, Pallas kernels for 0%

commit v1 on v0

v1 whole, which is shorter than its diff:
```python
import functools

import jax
import jax.numpy as jnp
from jax import lax
from jax.experimental import pallas as pl
from jax.experimental.pallas import tpu as pltpu
from jax.sharding import PartitionSpec as P

HD = 128
NBLK = 4
norm_eps = 1e-05
MESH = pl.DeviceIdType.MESH
F32 = jnp.float32
BF16 = jnp.bfloat16
TILE = 256


def dot_t(a, b):
    return lax.dot_general(a, b, (((1,), (1,)), ((), ())), preferred_element_type=F32)


def dot_0(a, b):
    return lax.dot_general(a, b, (((0,), (0,)), ((), ())), preferred_element_type=F32)


def kernel(
    S, T, N,
    pat_ref, hot_ref, fwd_ref, back_ref, grad_ref, gain_ref, wq_hbm, wo_hbm, kv_hbm,
    next_ref, prev_ref, kvg_ref, gg_ref,
    wq, wo, x, xg, bgb, kvb, kvs, hs1, hr1, qp, qr, ssp, ssr, q, qf, go,
    bl, blg, gqb, rts, rtr, hs2, hr2, pp, ppr, gp, gpr, ns, nr, ps, pr,
    w_sem, xs_sem, xr_sem, gs_sem, gr_sem, ks_sem, kr_sem, h1s_sem, h1r_sem,
    qs_sem, qr_sem, zs_sem, zr_sem, bs_sem, br_sem, gqs_sem, gqr_sem, rs_sem, rr_sem,
    h2s_sem, h2r_sem, kgs_sem, kgr_sem, pps_sem, ppr_sem, gps_sem, gpr_sem, sec_sem,
):
    s, t, d = lax.axis_index("section"), lax.axis_index("tensor"), lax.axis_index("dp")
    tok, W = fwd_ref.shape
    R = T // N
    RB = kv_hbm.shape[3]
    CH = T * S // NBLK
    heads = W // HD
    width = T * W

    def dev(os=0, ot=0, od=0):
        return (lax.rem(s + os, S), lax.rem(t + ot, T), lax.rem(d + od, N))

    pairs = [(os, ot) for ot in range(T) for os in range(S) if (os, ot) != (0, 0)]
    others = [(ot, od) for ot in range(T) for od in range(1, N)]
    barrier = pltpu.get_barrier_semaphore()
    for os, ot in pairs:
        pl.semaphore_signal(barrier, inc=1, device_id=dev(os, ot), device_id_type=MESH)
    for ot, od in others:
        pl.semaphore_signal(barrier, inc=1, device_id=dev(0, ot, od), device_id_type=MESH)

    wo_copy = pltpu.make_async_copy(wo_hbm, wo, w_sem.at[0])
    wq_copy = pltpu.make_async_copy(wq_hbm, wq, w_sem.at[1])
    wo_copy.start()
    wq_copy.start()
    x[pl.ds(0, tok)] = fwd_ref[...]
    x[pl.ds(tok, tok)] = back_ref[...]
    own = pl.ds(pl.multiple_of(d * tok, tok), tok)
    bgb[own] = grad_ref[...]
    pl.semaphore_wait(barrier, len(pairs) + len(others))

    sent = []

    def send(src, dst, ssem, rsem, device):
        copy = pltpu.make_async_remote_copy(
            src_ref=src, dst_ref=dst, send_sem=ssem, recv_sem=rsem,
            device_id=device, device_id_type=MESH,
        )
        copy.start()
        sent.append((None, copy))

    def send_or_keep(src, dst, ssem, rsem, device, here):
        copy = pltpu.make_async_remote_copy(
            src_ref=src, dst_ref=dst, send_sem=ssem, recv_sem=rsem,
            device_id=device, device_id_type=MESH,
        )

        @pl.when(here)
        def _():
            pltpu.make_async_copy(src, dst, rsem).start()

        @pl.when(jnp.logical_not(here))
        def _():
            copy.start()

        sent.append((jnp.logical_not(here), copy))

    def arrived(ref, sem):
        pltpu.make_async_copy(ref, ref, sem).wait()

    core = t // R
    part = lax.rem(t, R)
    slot = part * N + d

    def half_gather(src, dst, rows, ssem, rsem):
        at = pl.ds(pl.multiple_of(d * rows, rows), rows)
        for ot in range(T):
            tt = lax.rem(t + ot, T)
            device = (s, tt, core)
            if ot == 0:
                send_or_keep(src, dst.at[part, at], ssem.at[ot], rsem.at[slot], device, core == d)
            else:
                send(src, dst.at[part, at], ssem.at[ot], rsem.at[slot], device)

    def half_gather_wait(dst, rows, rsem):
        for i in range(R):
            for e in range(N):
                arrived(dst.at[i, pl.ds(e * rows, rows)], rsem.at[i * N + e])

    def half_scatter(src, dst, ssem, rsem):
        for i in range(R):
            for e in range(N):
                here = jnp.logical_and(R * d + i == t, d == e)
                send_or_keep(
                    src.at[i, pl.ds(e * tok, tok)], dst.at[t], ssem.at[i * N + e],
                    rsem.at[t], (s, R * d + i, e), here,
                )

    def half_scatter_wait(dst, rsem):
        for e in range(T):
            arrived(dst.at[e], rsem.at[e])

    half_gather(x, xg, 2 * tok, xs_sem, xr_sem)
    for od in range(1, N):
        send(grad_ref, bgb.at[own], gs_sem.at[od], gr_sem.at[od], dev(0, 0, od))
    chunk = t * S + s
    mine = kvb.at[chunk // CH, lax.rem(chunk, CH)]
    for os, ot in pairs:
        ss, tt, _ = dev(os, ot)
        send(kv_hbm.at[ss, tt], mine, ks_sem.at[os, ot], kr_sem.at[os, ot], (ss, tt, d))
    keep_kv = pltpu.make_async_copy(kv_hbm.at[s, t], mine, kr_sem.at[0, 0])
    keep_kv.start()

    for od in range(1, N):
        arrived(bgb.at[own], gr_sem.at[od])
    wo_copy.wait()
    for i in range(R):
        @pl.loop(0, W // TILE)
        def _(j):
            cols = pl.ds(pl.multiple_of(j * TILE, TILE), TILE)
            rows = pl.ds(pl.multiple_of(i * W + j * TILE, TILE), TILE)
            hs1[i, :, cols] = dot_t(bgb[...], wo[rows, :]).astype(BF16)
    half_scatter(hs1, hr1, h1s_sem, h1r_sem)

    wq_copy.wait()
    half_gather_wait(xg, 2 * tok, xr_sem)
    squares = None
    for i in range(R):
        wide = xg[i].astype(F32)
        term = jnp.sum(wide * wide, axis=-1, keepdims=True)
        squares = term if squares is None else squares + term
        gains = gain_ref[:, pl.ds(pl.multiple_of((d * R + i) * W, W), W)]
        xg[i] = (wide * gains).astype(BF16)
    ssp[...] = jnp.broadcast_to(squares, ssp.shape)

    @pl.loop(0, W // TILE)
    def _(j):
        cols = pl.ds(pl.multiple_of(j * TILE, TILE), TILE)
        total = None
        for i in range(R):
            term = jnp.dot(xg[i], wq[pl.ds(i * W, W), cols], preferred_element_type=F32)
            total = term if total is None else total + term
        qp[:, cols] = total

    def group(e, rows):
        return pl.ds(pl.multiple_of(e * rows, rows), rows)

    for od in range(1, N):
        e = lax.rem(d + od, N)
        send(qp.at[group(e, 2 * tok)], qr.at[od - 1], qs_sem.at[od], qr_sem.at[od], (s, t, e))
        send(ssp.at[group(e, 2 * tok)], ssr.at[od - 1], zs_sem.at[od], zr_sem.at[od], (s, t, e))
    total = qp[group(d, 2 * tok)]
    squares = ssp[group(d, 2 * tok)]
    for od in range(1, N):
        arrived(qr.at[od - 1], qr_sem.at[od])
        arrived(ssr.at[od - 1], zr_sem.at[od])
        total = total + qr[od - 1]
        squares = squares + ssr[od - 1]
    inv = lax.rsqrt(squares[:, :1] * (1.0 / width) + norm_eps)
    q[...] = (total * inv).astype(BF16)
    qf[...] = total[tok:]
    inv_back = inv[tok:]
    half_scatter_wait(hr1, h1r_sem)
    total = hr1[0].astype(F32)
    for e in range(1, T):
        total = total + hr1[e].astype(F32)
    go[...] = total.astype(BF16)

    scale = HD ** (-0.5)
    keep_kv.wait()
    for os, ot in pairs:
        arrived(mine, kr_sem.at[os, ot])

    def picked(m, kind, h):
        cols = pl.ds(h * HD, HD)
        return jnp.concatenate(
            [
                kvb[pat_ref[m * 2 + j], :, kind, :, cols].reshape(CH * RB, HD)
                for j in range(2)
            ],
            axis=0,
        )

    def softmax(scores):
        e = jnp.exp(scores - jnp.max(scores, axis=-1, keepdims=True))
        return e / jnp.sum(e, axis=-1, keepdims=True)

    for h in range(heads):
        cols = pl.ds(h * HD, HD)
        probs = softmax(dot_t(q[pl.ds(0, tok), cols], picked(0, 0, h)) * scale)
        bl[:, cols] = jnp.dot(
            probs.astype(BF16), picked(0, 1, h), preferred_element_type=F32
        ).astype(BF16)
    half_gather(bl, blg, tok, bs_sem, br_sem)

    row = jnp.zeros((tok, 1), F32)
    for h in range(heads):
        cols = pl.ds(h * HD, HD)
        keys, values = picked(1, 0, h), picked(1, 1, h)
        qh = q[pl.ds(tok, tok), cols]
        gh = go[:, cols]
        probs = softmax(dot_t(qh, keys) * scale)
        rounded = probs.astype(BF16)
        gv = dot_0(rounded, gh)
        gpr_h = dot_t(gh, values)
        gs = probs * (gpr_h - jnp.sum(gpr_h * probs, axis=-1, keepdims=True))
        scaled = (gs * scale).astype(BF16)
        gq = jnp.dot(scaled, keys, preferred_element_type=F32).astype(BF16)
        gk = dot_0(scaled, qh)
        gqb[own, cols] = gq
        row = row + jnp.sum(gq.astype(F32) * qf[:, cols], axis=-1, keepdims=True)
        half = CH * RB
        for b in range(NBLK):
            h0, h1 = hot_ref[b * 2], hot_ref[b * 2 + 1]
            for kind, g in ((0, gk), (1, gv)):
                kvs[b, :, kind, :, cols] = (
                    (g[:half] * h0 + g[half:] * h1).astype(BF16).reshape(CH, RB, HD)
                )
    rts[...] = jnp.broadcast_to(row, rts.shape)
    for od in range(1, N):
        send(gqb.at[own], gqb.at[own], gqs_sem.at[od], gqr_sem.at[od], dev(0, 0, od))
    for ot in range(1, T):
        send(rts, rtr.at[ot - 1], rs_sem.at[ot], rr_sem.at[ot], dev(0, ot, 0))

    def kv_back(os, ot):
        ss, tt, _ = dev(os, ot)
        c = tt * S + ss
        return kvs.at[c // CH, lax.rem(c, CH)], (ss, tt, d)

    def kv_send(which):
        for os, ot in which:
            src, device = kv_back(os, ot)
            send(src, kvg_ref.at[s, t], kgs_sem.at[os, ot], kgr_sem.at[os, ot], device)

    kv_send([p for p in pairs if p[1] == 0])
    keep_kvg = pltpu.make_async_copy(kv_back(0, 0)[0], kvg_ref.at[s, t], kgr_sem.at[0, 0])
    keep_kvg.start()

    for od in range(1, N):
        arrived(gqb.at[own], gqr_sem.at[od])
    for i in range(R):
        @pl.loop(0, W // TILE)
        def _(j):
            cols = pl.ds(pl.multiple_of(j * TILE, TILE), TILE)
            rows = pl.ds(pl.multiple_of(i * W + j * TILE, TILE), TILE)
            hs2[i, :, cols] = dot_t(gqb[...], wq[rows, :]).astype(BF16)
    half_scatter(hs2, hr2, h2s_sem, h2r_sem)
    kv_send([p for p in pairs if p[1] != 0])

    half_gather_wait(blg, tok, br_sem)

    @pl.loop(0, W // TILE)
    def _(j):
        cols = pl.ds(pl.multiple_of(j * TILE, TILE), TILE)
        total = None
        for i in range(R):
            term = jnp.dot(blg[i], wo[pl.ds(i * W, W), cols], preferred_element_type=F32)
            total = term if total is None else total + term
        pp[:, cols] = total

    for od in range(1, N):
        e = lax.rem(d + od, N)
        send(pp.at[group(e, tok)], ppr.at[od - 1], pps_sem.at[od], ppr_sem.at[od], (s, t, e))
    total = fwd_ref[...].astype(F32) + pp[own]
    for od in range(1, N):
        arrived(ppr.at[od - 1], ppr_sem.at[od])
        total = total + ppr[od - 1]
    ns[...] = total.astype(BF16)
    send(ns, nr, sec_sem.at[0], sec_sem.at[1], dev(1))

    for ot in range(1, T):
        arrived(rtr.at[ot - 1], rr_sem.at[ot])
        row = row + rtr[ot - 1][:, :1]
    half_scatter_wait(hr2, h2r_sem)
    gn = hr2[0].astype(F32)
    for e in range(1, T):
        gn = gn + hr2[e].astype(F32)
    back = back_ref[...].astype(F32)
    gains = gain_ref[:, pl.ds(pl.multiple_of(t * W, W), W)]
    gp[...] = jnp.sum(gn * back * inv_back, axis=0, keepdims=True)
    for od in range(1, N):
        send(gp, gpr.at[od - 1], gps_sem.at[od], gpr_sem.at[od], dev(0, 0, od))
    wide = grad_ref[...].astype(F32) + gains * inv_back * gn
    wide = wide - back * (inv_back * inv_back * inv_back * row * (1.0 / width))
    ps[...] = wide.astype(BF16)
    send(ps, pr, sec_sem.at[2], sec_sem.at[3], dev(S - 1))
    total = gp[...]
    for od in range(1, N):
        arrived(gpr.at[od - 1], gpr_sem.at[od])
        total = total + gpr[od - 1]
    gg_ref[...] = total
    arrived(nr, sec_sem.at[1])
    next_ref[...] = nr[...]
    arrived(pr, sec_sem.at[3])
    keep = jnp.where(s < S - 1, 1.0, 0.0).astype(F32)
    prev_ref[...] = (pr[...].astype(F32) * keep).astype(BF16)
    keep_kvg.wait()
    for os, ot in pairs:
        arrived(kvs.at[0, 0], kgr_sem.at[os, ot])
    for cond, copy in sent:
        if cond is None:
            copy.wait_send()
        else:
            pl.when(cond)(copy.wait_send)


def on_device(S, T, N, fwd_in, back_in, back_grad, gain, w_query, w_out, neighbour_kv, pattern):
    _, tok, W = fwd_in.shape
    rb = neighbour_kv.shape[1]
    D = gain.shape[1]
    half = w_query.shape[1]
    R = T // N
    CH = T * S // NBLK
    kv = neighbour_kv.reshape(S, rb, 2, T, W).transpose(0, 3, 2, 1, 4)
    picks = pattern.reshape(4)
    hot = (picks[2:][None, :] == jnp.arange(NBLK, dtype=jnp.int32)[:, None]).astype(F32).reshape(-1)
    vm = pl.BlockSpec(memory_space=pltpu.VMEM)
    sm = pl.BlockSpec(memory_space=pltpu.SMEM)
    hb = pl.BlockSpec(memory_space=pl.ANY)
    V = pltpu.VMEM
    dma = lambda *n: pltpu.SemaphoreType.DMA(n)
    M = max(N - 1, 1)
    scratch = [
        V((half, W), BF16), V((half, W), BF16),
        V((2 * tok, W), BF16), V((R, N * 2 * tok, W), BF16), V((N * tok, W), BF16),
        V((NBLK, CH, 2, rb, W), BF16), V((NBLK, CH, 2, rb, W), BF16),
        V((R, N * tok, W), BF16), V((T, tok, W), BF16),
        V((N * 2 * tok, W), F32), V((M, 2 * tok, W), F32),
        V((N * 2 * tok, 128), F32), V((M, 2 * tok, 128), F32),
        V((2 * tok, W), BF16), V((tok, W), F32), V((tok, W), BF16),
        V((tok, W), BF16), V((R, N * tok, W), BF16), V((N * tok, W), BF16),
        V((tok, 128), F32), V((T - 1, tok, 128), F32),
        V((R, N * tok, W), BF16), V((T, tok, W), BF16),
        V((N * tok, W), F32), V((M, tok, W), F32),
        V((1, W), F32), V((M, 1, W), F32),
        V((tok, W), BF16), V((tok, W), BF16), V((tok, W), BF16), V((tok, W), BF16),
        dma(2), dma(T), dma(R * N), dma(N), dma(N), dma(S, T), dma(S, T), dma(R * N), dma(T),
        dma(N), dma(N), dma(N), dma(N), dma(T), dma(R * N), dma(N), dma(N), dma(T), dma(T),
        dma(R * N), dma(T), dma(S, T), dma(S, T), dma(N), dma(N), dma(N), dma(N), dma(4),
    ]
    next_in, prev_grad, kvg, gg = pl.pallas_call(
        functools.partial(kernel, S, T, N),
        out_shape=[
            jax.ShapeDtypeStruct((tok, W), BF16),
            jax.ShapeDtypeStruct((tok, W), BF16),
            jax.ShapeDtypeStruct((S, T, 2, rb, W), BF16),
            jax.ShapeDtypeStruct((1, W), F32),
        ],
        in_specs=[sm, sm, vm, vm, vm, vm, hb, hb, hb],
        out_specs=[vm, vm, hb, vm],
        scratch_shapes=scratch,
        compiler_params=pltpu.CompilerParams(
            collective_id=0, has_side_effects=True, vmem_limit_bytes=48 * 2**20
        ),
        cost_estimate=pl.CostEstimate(
            flops=5 * 10**9, bytes_accessed=14 * 2**20, transcendentals=2 * 10**5
        ),
    )(picks, hot, fwd_in[0], back_in[0], back_grad[0], gain, w_query[0], w_out[0], kv)
    kv_grad = kvg.transpose(0, 3, 2, 1, 4).reshape(S, rb, 2, D)
    return (next_in[None], prev_grad[None], kv_grad, gg)


def solution(mesh):
    S, T, N = (mesh.shape[a] for a in ("section", "tensor", "dp"))
    return jax.shard_map(
        functools.partial(on_device, S, T, N),
        mesh=mesh,
        in_specs=(
            P("section", "dp", "tensor"),
            P("section", "dp", "tensor"),
            P("section", "dp", "tensor"),
            P("section", None),
            P("section", "dp", "tensor"),
            P("section", "dp", "tensor"),
            P(None, ("section", "tensor", "dp"), None, None),
            P(None, "dp", None),
        ),
        out_specs=(
            P("section", "dp", "tensor"),
            P("section", "dp", "tensor"),
            P(None, ("section", "tensor", "dp"), None, None),
            P("section", "tensor"),
        ),
        check_vma=False,
    )
```

time: 297 us -> 174 us (0.59)
  the two profiles are of different devices: /device:TPU:0 before, /device:TPU:27 now
where the time goes in v1:
time: 174 us
  Pallas kernels  160 us (92%)
  local copies, waits for them, and re-layouts  11.8 us (7%)
    pallas_call x1, Pallas kernels, on_device(): pl.pallas_call(functools.partial(kernel, S, T, N), out_shape=[jax.ShapeDt...  160 us
    unnamed x14, local copies, waits for them, and re-layouts  6.68 us
    reshape x2, local copies, waits for them, and re-layouts, on_device(): kv = neighbour_kv.reshape(S, rb, 2, T, W).transpose(0, 3, 2, 1, 4)  4.31 us

profile of v1, /device:TPU:27, one launch (start us, length us, event | category | flops | bytes accessed | tf_op | source)
XLA Modules:
  0.0 174.3 jit_solution(9136335763140951228)
XLA Ops:
  0.6 0.7 slice_bitcast_fusion
  1.3 0.5 broadcast.5
  1.8 1.3 reduce.3
  3.1 0.1 reshape.26.pat_ref
  3.2 0.1 reshape.29.hot_ref
  3.3 3.2 %reshape.30 = bf16[4,32,2,4,1024]{4,3,2,1,0:T(4,128)(2,1)S(1)} reshape(bf16[4,32,2,4096]{3,2,1,0:T(2,128)(2,1)} %param.14) | data formatting | bytes 4194304 | tf_op jit(solution)/shard_map/reshape | solution.py:338
  6.5 0.0 copy-start
  6.5 0.0 copy-start.1
  6.5 0.0 copy-start.2
  6.5 0.0 copy-start.3
  6.5 1.2 copy.21
  7.7 0.0 copy-done
  7.7 0.0 copy-done.1
  7.7 0.0 copy-done.2
  7.7 0.0 copy-done.3
  7.7 160.4 %shard_map.111 = (bf16[64,1024]{1,0:T(8,128)(2,1)S(1)}, bf16[64,1024]{1,0:T(8,128)(2,1)S(1)}, bf16[4,4,2,32,1024]{4,3,2,1,0:T(8,128)(2,1)S(1)}, f32[1,1024]{1,0:T(1,128)S(1)}) custom-call(s32[4]{0:T(128)S(1)} %reshape.26.pat_ref, f32[8]{0:T(128)S(1)} %reshape.29.hot_ref, bf16[64,1024]{1,0:T(8,128)(2,1)S(1)} %bitcast.17, bf16[64,1024]{1,0:T(8,128)(2,1)S(1)} %bitcast.18, ...), custom_call_target="tpu_custom_call" | custom-call | flops 5000000000 | bytes 14680064 | tf_op jit(solution)/shard_map/pallas_call | solution.py:365
  168.1 1.6 copy.18
  169.8 2.6 %reshape.31 = bf16[4,32,2,4096]{3,2,1,0:T(2,128)(2,1)} reshape(bf16[4,32,2,4,1024]{4,3,2,1,0:T(4,128)(2,1)S(1)} %copy.18) | data formatting | bytes 4194304
  172.4 0.7 copy.25
  173.0 0.7 copy.26
  173.7 0.6 copy.27
  (1 shorter events, 0.0 us)
Async XLA Ops:
  6.5 1.2 copy-start
  6.5 1.2 copy-start.1
  6.5 1.2 copy-start.2
  6.5 1.2 copy-start.3

commit v2 on v1

--- a/solution.py
+++ b/solution.py
@@ -26,30 +26,32 @@
 
 def kernel(
     S, T, N,
-    pat_ref, hot_ref, fwd_ref, back_ref, grad_ref, gain_ref, wq_hbm, wo_hbm, kv_hbm,
+    pat_ref, fwd_ref, back_ref, grad_ref, gain_ref, wq_hbm, wo_hbm, kv_hbm,
     next_ref, prev_ref, kvg_ref, gg_ref,
     wq, wo, x, xg, bgb, kvb, kvs, hs1, hr1, qp, qr, ssp, ssr, q, qf, go,
-    bl, blg, gqb, rts, rtr, hs2, hr2, pp, ppr, gp, gpr, ns, nr, ps, pr,
+    bl, blg, gqb, rts, rtr, hs2, hr2, qa, ga, ebuf, gbuf, obuf, st, sr, obs, obr, gqs, gqp, pp, ppr, gp, gpr, ns, nr, ps, pr,
     w_sem, xs_sem, xr_sem, gs_sem, gr_sem, ks_sem, kr_sem, h1s_sem, h1r_sem,
     qs_sem, qr_sem, zs_sem, zr_sem, bs_sem, br_sem, gqs_sem, gqr_sem, rs_sem, rr_sem,
     h2s_sem, h2r_sem, kgs_sem, kgr_sem, pps_sem, ppr_sem, gps_sem, gpr_sem, sec_sem,
+    qas_sem, qar_sem, gas_sem, gar_sem, sts_sem, str_sem, obs_sem, obr_sem, gqps_sem, gqpr_sem,
 ):
     s, t, d = lax.axis_index("section"), lax.axis_index("tensor"), lax.axis_index("dp")
     tok, W = fwd_ref.shape
     R = T // N
-    RB = kv_hbm.shape[3]
-    CH = T * S // NBLK
+    RB = kv_hbm.shape[2]
     heads = W // HD
+    H = T * heads
+    rows_here = S * RB
     width = T * W
 
     def dev(os=0, ot=0, od=0):
         return (lax.rem(s + os, S), lax.rem(t + ot, T), lax.rem(d + od, N))
 
-    pairs = [(os, ot) for ot in range(T) for os in range(S) if (os, ot) != (0, 0)]
-    others = [(ot, od) for ot in range(T) for od in range(1, N)]
+    pairs = list(range(1, S))
+    others = [(ot, od) for ot in range(T) for od in range(N) if (ot, od) != (0, 0)]
     barrier = pltpu.get_barrier_semaphore()
-    for os, ot in pairs:
-        pl.semaphore_signal(barrier, inc=1, device_id=dev(os, ot), device_id_type=MESH)
+    for os in pairs:
+        pl.semaphore_signal(barrier, inc=1, device_id=dev(os), device_id_type=MESH)
     for ot, od in others:
         pl.semaphore_signal(barrier, inc=1, device_id=dev(0, ot, od), device_id_type=MESH)
 
@@ -127,12 +129,10 @@
     half_gather(x, xg, 2 * tok, xs_sem, xr_sem)
     for od in range(1, N):
         send(grad_ref, bgb.at[own], gs_sem.at[od], gr_sem.at[od], dev(0, 0, od))
-    chunk = t * S + s
-    mine = kvb.at[chunk // CH, lax.rem(chunk, CH)]
-    for os, ot in pairs:
-        ss, tt, _ = dev(os, ot)
-        send(kv_hbm.at[ss, tt], mine, ks_sem.at[os, ot], kr_sem.at[os, ot], (ss, tt, d))
-    keep_kv = pltpu.make_async_copy(kv_hbm.at[s, t], mine, kr_sem.at[0, 0])
+    for os in pairs:
+        ss, _, _ = dev(os)
+        send(kv_hbm.at[ss], kvb.at[s], ks_sem.at[os], kr_sem.at[os], dev(os))
+    keep_kv = pltpu.make_async_copy(kv_hbm.at[s], kvb.at[s], kr_sem.at[0])
     keep_kv.start()
 
     for od in range(1, N):
@@ -184,81 +184,125 @@
     q[...] = (total * inv).astype(BF16)
     qf[...] = total[tok:]
     inv_back = inv[tok:]
+    qa[0] = q[...]
+    for ot in range(1, T):
+        send(q, qa.at[ot], qas_sem.at[ot], qar_sem.at[ot], dev(0, ot))
     half_scatter_wait(hr1, h1r_sem)
     total = hr1[0].astype(F32)
     for e in range(1, T):
         total = total + hr1[e].astype(F32)
     go[...] = total.astype(BF16)
+    ga[0] = go[...]
+    for ot in range(1, T):
+        send(go, ga.at[ot], gas_sem.at[ot], gar_sem.at[ot], dev(0, ot))
 
     scale = HD ** (-0.5)
+    block = t * NBLK // T
+    counts = []
+    for m in range(2):
+        count = jnp.float32(0.0)
+        for j in range(2):
+            count = count + jnp.where(pat_ref[m * 2 + j] == block, 1.0, 0.0).astype(F32)
+        counts.append(count)
+    is_fwd = lax.broadcasted_iota(jnp.int32, (2 * tok, 1), 0) < tok
+    times = jnp.where(is_fwd, counts[0], counts[1])
+    lane = lax.broadcasted_iota(jnp.int32, (2 * tok, 128), 1)
     keep_kv.wait()
-    for os, ot in pairs:
-        arrived(mine, kr_sem.at[os, ot])
-
-    def picked(m, kind, h):
-        cols = pl.ds(h * HD, HD)
-        return jnp.concatenate(
-            [
-                kvb[pat_ref[m * 2 + j], :, kind, :, cols].reshape(CH * RB, HD)
-                for j in range(2)
-            ],
-            axis=0,
-        )
-
-    def softmax(scores):
-        e = jnp.exp(scores - jnp.max(scores, axis=-1, keepdims=True))
-        return e / jnp.sum(e, axis=-1, keepdims=True)
-
-    for h in range(heads):
-        cols = pl.ds(h * HD, HD)
-        probs = softmax(dot_t(q[pl.ds(0, tok), cols], picked(0, 0, h)) * scale)
-        bl[:, cols] = jnp.dot(
-            probs.astype(BF16), picked(0, 1, h), preferred_element_type=F32
-        ).astype(BF16)
+    for os in pairs:
+        arrived(kvb.at[s], kr_sem.at[os])
+
+    def kv_rows(kind, cols):
+        return kvb[:, kind, :, cols].reshape(rows_here, HD)
+
+    stats = jnp.zeros((2 * tok, 128), F32)
+    for ot in range(T):
+        if ot:
+            arrived(q, qar_sem.at[ot])
+            arrived(go, gar_sem.at[ot])
+        tt = lax.rem(t + T - ot, T)
+        for h in range(heads):
+            g = tt * heads + h
+            cols = pl.ds(pl.multiple_of(g * HD, HD), HD)
+            at = pl.ds(h * HD, HD)
+            keys, values = kv_rows(0, cols), kv_rows(1, cols)
+            scores = dot_t(qa[ot, :, at], keys) * scale
+            top = jnp.max(scores, axis=-1, keepdims=True)
+            e = jnp.exp(scores - top) * times
+            gprob = dot_t(ga[ot, :, at], values)
+            obuf[g] = jnp.dot(e[:tok].astype(BF16), values, preferred_element_type=F32)
+            ebuf[g] = e[tok:]
+            gbuf[g] = gprob
+            mass = jnp.sum(e, axis=-1, keepdims=True)
+            delta = jnp.sum(e[tok:] * gprob, axis=-1, keepdims=True)
+            delta = jnp.concatenate([jnp.zeros_like(delta), delta], axis=0)
+            top = jnp.where(times > 0.0, top, -1e30)
+            stats = jnp.where(lane == g, top, stats)
+            stats = jnp.where(lane == g + H, mass, stats)
+            stats = jnp.where(lane == g + 2 * H, delta, stats)
+    st[...] = stats
+    for ot in range(1, T):
+        send(st, sr.at[ot - 1], sts_sem.at[ot], str_sem.at[ot], dev(0, ot))
+    for ot in range(1, T):
+        arrived(st, str_sem.at[ot])
+    every = [stats] + [sr[ot - 1] for ot in range(1, T)]
+    top = every[0][:, :H]
+    for v in every[1:]:
+        top = jnp.maximum(top, v[:, :H])
+    mass = jnp.zeros((2 * tok, H), F32)
+    delta = jnp.zeros((2 * tok, H), F32)
+    for v in every:
+        weight = jnp.exp(v[:, :H] - top)
+        mass = mass + weight * v[:, H:2 * H]
+        delta = delta + weight * v[:, 2 * H:3 * H]
+    alpha = jnp.exp(stats[:, :H] - top) / mass
+    delta = delta / mass
+
+    def scatter(src, dst, e, ssem, rsem):
+        send_or_keep(src.at[e], dst.at[t], ssem.at[e], rsem.at[t], (s, e, d), t == e)
+
+    for e in range(T):
+        for h in range(heads):
+            g = e * heads + h
+            obs[e, :, pl.ds(h * HD, HD)] = (obuf[g] * alpha[:tok, g:g + 1]).astype(BF16)
+        scatter(obs, obr, e, obs_sem, obr_sem)
+    for e in range(T):
+        slot_of = lax.rem(t + T - e, T)
+        for h in range(heads):
+            g = e * heads + h
+            cols, at = pl.ds(g * HD, HD), pl.ds(h * HD, HD)
+            keys = kv_rows(0, cols)
+            probs = ebuf[g] * alpha[tok:, g:g + 1]
+            gv = dot_0(probs.astype(BF16), ga[slot_of, :, at])
+            gs = probs * (gbuf[g] - delta[tok:, g:g + 1])
+            scaled = (gs * scale).astype(BF16)
+            gqs[e, :, at] = jnp.dot(scaled, keys, preferred_element_type=F32).astype(BF16)
+            gk = dot_0(scaled, qa[slot_of, pl.ds(tok, tok), at])
+            kvs[:, 0, :, cols] = gk.astype(BF16).reshape(S, RB, HD)
+            kvs[:, 1, :, cols] = gv.astype(BF16).reshape(S, RB, HD)
+        scatter(gqs, gqp, e, gqps_sem, gqpr_sem)
+    for os in pairs:
+        ss, _, _ = dev(os)
+        send(kvs.at[ss], kvg_ref.at[s], kgs_sem.at[os], kgr_sem.at[os], dev(os))
+    keep_kvg = pltpu.make_async_copy(kvs.at[s], kvg_ref.at[s], kgr_sem.at[0])
+    keep_kvg.start()
+
+    half_scatter_wait(obr, obr_sem)
+    total = obr[0].astype(F32)
+    for e in range(1, T):
+        total = total + obr[e].astype(F32)
+    bl[...] = total.astype(BF16)
     half_gather(bl, blg, tok, bs_sem, br_sem)
-
-    row = jnp.zeros((tok, 1), F32)
-    for h in range(heads):
-        cols = pl.ds(h * HD, HD)
-        keys, values = picked(1, 0, h), picked(1, 1, h)
-        qh = q[pl.ds(tok, tok), cols]
-        gh = go[:, cols]
-        probs = softmax(dot_t(qh, keys) * scale)
-        rounded = probs.astype(BF16)
-        gv = dot_0(rounded, gh)
-        gpr_h = dot_t(gh, values)
-        gs = probs * (gpr_h - jnp.sum(gpr_h * probs, axis=-1, keepdims=True))
-        scaled = (gs * scale).astype(BF16)
-        gq = jnp.dot(scaled, keys, preferred_element_type=F32).astype(BF16)
-        gk = dot_0(scaled, qh)
-        gqb[own, cols] = gq
-        row = row + jnp.sum(gq.astype(F32) * qf[:, cols], axis=-1, keepdims=True)
-        half = CH * RB
-        for b in range(NBLK):
-            h0, h1 = hot_ref[b * 2], hot_ref[b * 2 + 1]
-            for kind, g in ((0, gk), (1, gv)):
-                kvs[b, :, kind, :, cols] = (
-                    (g[:half] * h0 + g[half:] * h1).astype(BF16).reshape(CH, RB, HD)
-                )
+    half_scatter_wait(gqp, gqpr_sem)
+    total = gqp[0].astype(F32)
+    for e in range(1, T):
+        total = total + gqp[e].astype(F32)
+    gqb[own] = total.astype(BF16)
+    for od in range(1, N):
+        send(gqb.at[own], gqb.at[own], gqs_sem.at[od], gqr_sem.at[od], dev(0, 0, od))
+    row = jnp.sum(total * qf[...], axis=-1, keepdims=True)
     rts[...] = jnp.broadcast_to(row, rts.shape)
-    for od in range(1, N):
-        send(gqb.at[own], gqb.at[own], gqs_sem.at[od], gqr_sem.at[od], dev(0, 0, od))
     for ot in range(1, T):
         send(rts, rtr.at[ot - 1], rs_sem.at[ot], rr_sem.at[ot], dev(0, ot, 0))
-
-    def kv_back(os, ot):
-        ss, tt, _ = dev(os, ot)
-        c = tt * S + ss
-        return kvs.at[c // CH, lax.rem(c, CH)], (ss, tt, d)
-
-    def kv_send(which):
-        for os, ot in which:
-            src, device = kv_back(os, ot)
-            send(src, kvg_ref.at[s, t], kgs_sem.at[os, ot], kgr_sem.at[os, ot], device)
-
-    kv_send([p for p in pairs if p[1] == 0])
-    keep_kvg = pltpu.make_async_copy(kv_back(0, 0)[0], kvg_ref.at[s, t], kgr_sem.at[0, 0])
-    keep_kvg.start()
 
     for od in range(1, N):
         arrived(gqb.at[own], gqr_sem.at[od])
@@ -269,7 +313,6 @@
             rows = pl.ds(pl.multiple_of(i * W + j * TILE, TILE), TILE)
             hs2[i, :, cols] = dot_t(gqb[...], wq[rows, :]).astype(BF16)
     half_scatter(hs2, hr2, h2s_sem, h2r_sem)
-    kv_send([p for p in pairs if p[1] != 0])
 
     half_gather_wait(blg, tok, br_sem)
 
@@ -319,8 +362,8 @@
     keep = jnp.where(s < S - 1, 1.0, 0.0).astype(F32)
     prev_ref[...] = (pr[...].astype(F32) * keep).astype(BF16)
     keep_kvg.wait()
-    for os, ot in pairs:
-        arrived(kvs.at[0, 0], kgr_sem.at[os, ot])
+    for os in pairs:
+        arrived(kvs.at[0], kgr_sem.at[os])
     for cond, copy in sent:
         if cond is None:
             copy.wait_send()
@@ -334,10 +377,9 @@
     D = gain.shape[1]
     half = w_query.shape[1]
     R = T // N
-    CH = T * S // NBLK
-    kv = neighbour_kv.reshape(S, rb, 2, T, W).transpose(0, 3, 2, 1, 4)
+    H = D // HD
+    kv = neighbour_kv.transpose(0, 2, 1, 3)
     picks = pattern.reshape(4)
-    hot = (picks[2:][None, :] == jnp.arange(NBLK, dtype=jnp.int32)[:, None]).astype(F32).reshape(-1)
     vm = pl.BlockSpec(memory_space=pltpu.VMEM)
     sm = pl.BlockSpec(memory_space=pltpu.SMEM)
     hb = pl.BlockSpec(memory_space=pl.ANY)
@@ -347,7 +389,7 @@
     scratch = [
         V((half, W), BF16), V((half, W), BF16),
         V((2 * tok, W), BF16), V((R, N * 2 * tok, W), BF16), V((N * tok, W), BF16),
-        V((NBLK, CH, 2, rb, W), BF16), V((NBLK, CH, 2, rb, W), BF16),
+        V((S, 2, rb, D), BF16), V((S, 2, rb, D), BF16),
         V((R, N * tok, W), BF16), V((T, tok, W), BF16),
         V((N * 2 * tok, W), F32), V((M, 2 * tok, W), F32),
         V((N * 2 * tok, 128), F32), V((M, 2 * tok, 128), F32),
@@ -355,22 +397,27 @@
         V((tok, W), BF16), V((R, N * tok, W), BF16), V((N * tok, W), BF16),
         V((tok, 128), F32), V((T - 1, tok, 128), F32),
         V((R, N * tok, W), BF16), V((T, tok, W), BF16),
+        V((T, 2 * tok, W), BF16), V((T, tok, W), BF16),
+        V((H, tok, S * rb), F32), V((H, tok, S * rb), F32), V((H, tok, HD), F32),
+        V((2 * tok, 128), F32), V((T - 1, 2 * tok, 128), F32),
+        V((T, tok, W), BF16), V((T, tok, W), BF16), V((T, tok, W), BF16), V((T, tok, W), BF16),
         V((N * tok, W), F32), V((M, tok, W), F32),
         V((1, W), F32), V((M, 1, W), F32),
         V((tok, W), BF16), V((tok, W), BF16), V((tok, W), BF16), V((tok, W), BF16),
-        dma(2), dma(T), dma(R * N), dma(N), dma(N), dma(S, T), dma(S, T), dma(R * N), dma(T),
+        dma(2), dma(T), dma(R * N), dma(N), dma(N), dma(S), dma(S), dma(R * N), dma(T),
         dma(N), dma(N), dma(N), dma(N), dma(T), dma(R * N), dma(N), dma(N), dma(T), dma(T),
-        dma(R * N), dma(T), dma(S, T), dma(S, T), dma(N), dma(N), dma(N), dma(N), dma(4),
+        dma(R * N), dma(T), dma(S), dma(S), dma(N), dma(N), dma(N), dma(N), dma(4),
+        dma(T), dma(T), dma(T), dma(T), dma(T), dma(T), dma(T), dma(T), dma(T), dma(T),
     ]
     next_in, prev_grad, kvg, gg = pl.pallas_call(
         functools.partial(kernel, S, T, N),
         out_shape=[
             jax.ShapeDtypeStruct((tok, W), BF16),
             jax.ShapeDtypeStruct((tok, W), BF16),
-            jax.ShapeDtypeStruct((S, T, 2, rb, W), BF16),
+            jax.ShapeDtypeStruct((S, 2, rb, D), BF16),
             jax.ShapeDtypeStruct((1, W), F32),
         ],
-        in_specs=[sm, sm, vm, vm, vm, vm, hb, hb, hb],
+        in_specs=[sm, vm, vm, vm, vm, hb, hb, hb],
         out_specs=[vm, vm, hb, vm],
         scratch_shapes=scratch,
         compiler_params=pltpu.CompilerParams(
@@ -379,8 +426,8 @@
         cost_estimate=pl.CostEstimate(
             flops=5 * 10**9, bytes_accessed=14 * 2**20, transcendentals=2 * 10**5
         ),
-    )(picks, hot, fwd_in[0], back_in[0], back_grad[0], gain, w_query[0], w_out[0], kv)
-    kv_grad = kvg.transpose(0, 3, 2, 1, 4).reshape(S, rb, 2, D)
+    )(picks, fwd_in[0], back_in[0], back_grad[0], gain, w_query[0], w_out[0], kv)
+    kv_grad = kvg.transpose(0, 2, 1, 3)
     return (next_in[None], prev_grad[None], kv_grad, gg)
 
 

time: 174 us -> 149 us (0.86)
  the two profiles are of different devices: /device:TPU:27 before, /device:TPU:0 now
where the time goes in v2:
time: 149 us; the launch traced here: 148 us
  Pallas kernels  137 us (92%)
  local copies, waits for them, and re-layouts  8.97 us (6%)
    pallas_call x1, Pallas kernels, on_device(): pl.pallas_call(functools.partial(kernel, S, T, N), out_shape=[jax.ShapeDt...  137 us
    unnamed x14, local copies, waits for them, and re-layouts  8.89 us

profile of v2, /device:TPU:0, one launch (start us, length us, event | category | flops | bytes accessed | tf_op | source)
XLA Modules:
  0.0 147.5 jit_solution(11790288001732502102)
XLA Ops:
  0.6 0.5 broadcast.3
  1.1 1.3 reduce.3
  2.5 0.1 reshape.11.pat_ref
  2.6 0.0 copy-start
  2.6 0.0 copy-start.1
  2.6 0.0 copy-start.2
  2.6 0.0 copy-start.3
  2.6 3.0 %copy.15 = bf16[4,32,2,4096]{3,1,2,0:T(8,128)(2,1)S(1)} copy(bf16[4,32,2,4096]{3,2,1,0:T(2,128)(2,1)} %param.14) | data formatting | bytes 4194304 | tf_op args[6]
  5.5 0.0 copy-done
  5.5 0.0 copy-done.1
  5.6 0.0 copy-done.2
  5.6 0.0 copy-done.3
  5.6 136.5 %shard_map.111 = (bf16[64,1024]{1,0:T(8,128)(2,1)S(1)}, bf16[64,1024]{1,0:T(8,128)(2,1)S(1)}, bf16[4,2,32,4096]{3,2,1,0:T(8,128)(2,1)S(1)}, f32[1,1024]{1,0:T(1,128)S(1)}) custom-call(s32[4]{0:T(128)S(1)} %reshape.11.pat_ref, bf16[64,1024]{1,0:T(8,128)(2,1)S(1)} %bitcast.15, bf16[64,1024]{1,0:T(8,128)(2,1)S(1)} %bitcast.16, bf16[64,1024]{1,0:T(8,128)(2,1)S(1)} %bitcast.17, ...), custom_call_target="tpu_custom_call" | custom-call | flops 5000000000 | bytes 14680064 | tf_op jit(solution)/shard_map/pallas_call | solution.py:412
  142.1 3.5 %copy.13 = bf16[4,32,2,4096]{3,2,1,0:T(2,128)(2,1)} copy(bf16[4,32,2,4096]{3,1,2,0:T(8,128)(2,1)S(1)} %bitcast.11) | data formatting | bytes 4194304
  145.6 0.7 copy.19
  146.3 0.7 copy.20
  146.9 0.6 copy.21
Async XLA Ops:
  2.6 3.0 %copy-start = (bf16[1,64,1024]{2,1,0:T(8,128)(2,1)S(1)}, bf16[1,64,1024]{2,1,0:T(8,128)(2,1)}, u32[]{:S(2)}) copy-start(bf16[1,64,1024]{2,1,0:T(8,128)(2,1)} %param.8) | copy-start | bytes 393220
  2.6 3.0 %copy-start.1 = (bf16[1,64,1024]{2,1,0:T(8,128)(2,1)S(1)}, bf16[1,64,1024]{2,1,0:T(8,128)(2,1)}, u32[]{:S(2)}) copy-start(bf16[1,64,1024]{2,1,0:T(8,128)(2,1)} %param.9) | copy-start | bytes 393220
  2.6 3.0 %copy-start.2 = (bf16[1,64,1024]{2,1,0:T(8,128)(2,1)S(1)}, bf16[1,64,1024]{2,1,0:T(8,128)(2,1)}, u32[]{:S(2)}) copy-start(bf16[1,64,1024]{2,1,0:T(8,128)(2,1)} %param.10) | copy-start | bytes 393220
  2.6 3.0 %copy-start.3 = (f32[1,4096]{1,0:T(1,128)S(1)}, f32[1,4096]{1,0:T(1,128)}, u32[]{:S(2)}) copy-start(f32[1,4096]{1,0:T(1,128)} %gain_ref.1) | copy-start | bytes 49156

commit v3 on v2

--- a/solution.py
+++ b/solution.py
@@ -28,7 +28,7 @@
     S, T, N,
     pat_ref, fwd_ref, back_ref, grad_ref, gain_ref, wq_hbm, wo_hbm, kv_hbm,
     next_ref, prev_ref, kvg_ref, gg_ref,
-    wq, wo, x, xg, bgb, kvb, kvs, hs1, hr1, qp, qr, ssp, ssr, q, qf, go,
+    wq, wo, x, xg, hg, bgb, kvb, kvs, hs1, hr1, qp, qr, ssp, ssr, q, qf, go,
     bl, blg, gqb, rts, rtr, hs2, hr2, qa, ga, ebuf, gbuf, obuf, st, sr, obs, obr, gqs, gqp, pp, ppr, gp, gpr, ns, nr, ps, pr,
     w_sem, xs_sem, xr_sem, gs_sem, gr_sem, ks_sem, kr_sem, h1s_sem, h1r_sem,
     qs_sem, qr_sem, zs_sem, zr_sem, bs_sem, br_sem, gqs_sem, gqr_sem, rs_sem, rr_sem,
@@ -91,6 +91,22 @@
 
         sent.append((jnp.logical_not(here), copy))
 
+    def send_if(cond, src, dst, ssem, rsem, device):
+        copy = pltpu.make_async_remote_copy(
+            src_ref=src, dst_ref=dst, send_sem=ssem, recv_sem=rsem,
+            device_id=device, device_id_type=MESH,
+        )
+        pl.when(cond)(copy.start)
+        sent.append((cond, copy))
+
+    relay = T == 4 and N == 2
+
+    def direct(ot):
+        ends = jnp.logical_or(
+            jnp.logical_and(t == 0, ot == T - 1), jnp.logical_and(t == T - 1, ot == 1)
+        )
+        return jnp.logical_not(ends)
+
     def arrived(ref, sem):
         pltpu.make_async_copy(ref, ref, sem).wait()
 
@@ -105,13 +121,23 @@
             device = (s, tt, core)
             if ot == 0:
                 send_or_keep(src, dst.at[part, at], ssem.at[ot], rsem.at[slot], device, core == d)
+            elif relay and ot != 2:
+                send_if(direct(ot), src, dst.at[part, at], ssem.at[ot], rsem.at[slot], device)
             else:
                 send(src, dst.at[part, at], ssem.at[ot], rsem.at[slot], device)
 
-    def half_gather_wait(dst, rows, rsem):
-        for i in range(R):
+    def half_gather_wait(dst, rows, ssem, rsem):
+        relayed = relay and N == 2
+        order = [d, 1 - d] if relayed else list(range(R))
+        for k, i in enumerate(order):
             for e in range(N):
-                arrived(dst.at[i, pl.ds(e * rows, rows)], rsem.at[i * N + e])
+                ref = dst.at[i, pl.ds(e * rows, rows)]
+                arrived(ref, rsem.at[i * N + e])
+                if relayed and k == 0:
+                    send_if(
+                        t == 2 - d, ref, ref, ssem.at[T + e], rsem.at[i * N + e],
+                        (s, 3 * (1 - d), d),
+                    )
 
     def half_scatter(src, dst, ssem, rsem):
         for i in range(R):
@@ -147,14 +173,14 @@
     half_scatter(hs1, hr1, h1s_sem, h1r_sem)
 
     wq_copy.wait()
-    half_gather_wait(xg, 2 * tok, xr_sem)
+    half_gather_wait(xg, 2 * tok, xs_sem, xr_sem)
     squares = None
     for i in range(R):
         wide = xg[i].astype(F32)
         term = jnp.sum(wide * wide, axis=-1, keepdims=True)
         squares = term if squares is None else squares + term
         gains = gain_ref[:, pl.ds(pl.multiple_of((d * R + i) * W, W), W)]
-        xg[i] = (wide * gains).astype(BF16)
+        hg[i] = (wide * gains).astype(BF16)
     ssp[...] = jnp.broadcast_to(squares, ssp.shape)
 
     @pl.loop(0, W // TILE)
@@ -162,7 +188,7 @@
         cols = pl.ds(pl.multiple_of(j * TILE, TILE), TILE)
         total = None
         for i in range(R):
-            term = jnp.dot(xg[i], wq[pl.ds(i * W, W), cols], preferred_element_type=F32)
+            term = jnp.dot(hg[i], wq[pl.ds(i * W, W), cols], preferred_element_type=F32)
             total = term if total is None else total + term
         qp[:, cols] = total
 
@@ -184,9 +210,24 @@
     q[...] = (total * inv).astype(BF16)
     qf[...] = total[tok:]
     inv_back = inv[tok:]
+    def gather_send(src, dst, ot, ssem, rsem):
+        if relay and ot != 2:
+            send_if(direct(ot), src, dst.at[ot], ssem.at[ot], rsem.at[ot], dev(0, ot))
+        else:
+            send(src, dst.at[ot], ssem.at[ot], rsem.at[ot], dev(0, ot))
+
+    def gather_wait(dst, ot, ssem, rsem):
+        arrived(dst.at[ot], rsem.at[ot])
+        if relay and ot == 2:
+            to = jnp.where(t == 2, 3, 1)
+            send_if(
+                jnp.logical_or(t == 1, t == 2), dst.at[2], dst.at[to], ssem.at[0],
+                rsem.at[to], (s, jnp.where(t == 2, 3, 0), d),
+            )
+
     qa[0] = q[...]
     for ot in range(1, T):
-        send(q, qa.at[ot], qas_sem.at[ot], qar_sem.at[ot], dev(0, ot))
+        gather_send(q, qa, ot, qas_sem, qar_sem)
     half_scatter_wait(hr1, h1r_sem)
     total = hr1[0].astype(F32)
     for e in range(1, T):
@@ -194,7 +235,7 @@
     go[...] = total.astype(BF16)
     ga[0] = go[...]
     for ot in range(1, T):
-        send(go, ga.at[ot], gas_sem.at[ot], gar_sem.at[ot], dev(0, ot))
+        gather_send(go, ga, ot, gas_sem, gar_sem)
 
     scale = HD ** (-0.5)
     block = t * NBLK // T
@@ -202,7 +243,7 @@
     for m in range(2):
         count = jnp.float32(0.0)
         for j in range(2):
-            count = count + jnp.where(pat_ref[m * 2 + j] == block, 1.0, 0.0).astype(F32)
+            count = count + jnp.where(pat_ref[m, 0, j] == block, 1.0, 0.0).astype(F32)
         counts.append(count)
     is_fwd = lax.broadcasted_iota(jnp.int32, (2 * tok, 1), 0) < tok
     times = jnp.where(is_fwd, counts[0], counts[1])
@@ -215,10 +256,10 @@
         return kvb[:, kind, :, cols].reshape(rows_here, HD)
 
     stats = jnp.zeros((2 * tok, 128), F32)
-    for ot in range(T):
+    for ot in [0, 2, 1, 3] if relay else range(T):
         if ot:
-            arrived(q, qar_sem.at[ot])
-            arrived(go, gar_sem.at[ot])
+            gather_wait(qa, ot, qas_sem, qar_sem)
+            gather_wait(ga, ot, gas_sem, gar_sem)
         tt = lax.rem(t + T - ot, T)
         for h in range(heads):
             g = tt * heads + h
@@ -314,7 +355,7 @@
             hs2[i, :, cols] = dot_t(gqb[...], wq[rows, :]).astype(BF16)
     half_scatter(hs2, hr2, h2s_sem, h2r_sem)
 
-    half_gather_wait(blg, tok, br_sem)
+    half_gather_wait(blg, tok, bs_sem, br_sem)
 
     @pl.loop(0, W // TILE)
     def _(j):
@@ -379,7 +420,6 @@
     R = T // N
     H = D // HD
     kv = neighbour_kv.transpose(0, 2, 1, 3)
-    picks = pattern.reshape(4)
     vm = pl.BlockSpec(memory_space=pltpu.VMEM)
     sm = pl.BlockSpec(memory_space=pltpu.SMEM)
     hb = pl.BlockSpec(memory_space=pl.ANY)
@@ -388,7 +428,8 @@
     M = max(N - 1, 1)
     scratch = [
         V((half, W), BF16), V((half, W), BF16),
-        V((2 * tok, W), BF16), V((R, N * 2 * tok, W), BF16), V((N * tok, W), BF16),
+        V((2 * tok, W), BF16), V((R, N * 2 * tok, W), BF16), V((R, N * 2 * tok, W), BF16),
+        V((N * tok, W), BF16),
         V((S, 2, rb, D), BF16), V((S, 2, rb, D), BF16),
         V((R, N * tok, W), BF16), V((T, tok, W), BF16),
         V((N * 2 * tok, W), F32), V((M, 2 * tok, W), F32),
@@ -404,8 +445,8 @@
         V((N * tok, W), F32), V((M, tok, W), F32),
         V((1, W), F32), V((M, 1, W), F32),
         V((tok, W), BF16), V((tok, W), BF16), V((tok, W), BF16), V((tok, W), BF16),
-        dma(2), dma(T), dma(R * N), dma(N), dma(N), dma(S), dma(S), dma(R * N), dma(T),
-        dma(N), dma(N), dma(N), dma(N), dma(T), dma(R * N), dma(N), dma(N), dma(T), dma(T),
+        dma(2), dma(T + N), dma(R * N), dma(N), dma(N), dma(S), dma(S), dma(R * N), dma(T),
+        dma(N), dma(N), dma(N), dma(N), dma(T + N), dma(R * N), dma(N), dma(N), dma(T), dma(T),
         dma(R * N), dma(T), dma(S), dma(S), dma(N), dma(N), dma(N), dma(N), dma(4),
         dma(T), dma(T), dma(T), dma(T), dma(T), dma(T), dma(T), dma(T), dma(T), dma(T),
     ]
@@ -426,7 +467,7 @@
         cost_estimate=pl.CostEstimate(
             flops=5 * 10**9, bytes_accessed=14 * 2**20, transcendentals=2 * 10**5
         ),
-    )(picks, fwd_in[0], back_in[0], back_grad[0], gain, w_query[0], w_out[0], kv)
+    )(pattern, fwd_in[0], back_in[0], back_grad[0], gain, w_query[0], w_out[0], kv)
     kv_grad = kvg.transpose(0, 2, 1, 3)
     return (next_in[None], prev_grad[None], kv_grad, gg)
 

time: 149 us -> 137 us (0.919); the launches traced: 148 us -> 137 us
  Pallas kernels: 137 us -> 128 us
    pallas_call x1, Pallas kernels: 137 us -> 128 us  [on_device(): pl.pallas_call(functools.partial(kernel, S, T, N), out_shape=[jax.ShapeDt...]
    unnamed x14 -> x15, local copies, waits for them, and re-layouts: 8.89 us -> 8.4 us
where the time goes in v3:
time: 137 us
  Pallas kernels  128 us (93%)
  local copies, waits for them, and re-layouts  8.4 us (6%)
    pallas_call x1, Pallas kernels, on_device(): pl.pallas_call(functools.partial(kernel, S, T, N), out_shape=[jax.ShapeDt...  128 us
    unnamed x15, local copies, waits for them, and re-layouts  8.4 us

profile of v3, /device:TPU:0, one launch (start us, length us, event | category | flops | bytes accessed | tf_op | source)
XLA Modules:
  0.0 137.1 jit_solution(12360062715808544178)
XLA Ops:
  0.6 0.0 copy-start
  0.6 0.0 copy-start.1
  0.7 0.0 copy-start.2
  0.7 0.0 copy-start.3
  0.7 0.0 copy-start.4
  0.7 3.0 %copy.15 = bf16[4,32,2,4096]{3,1,2,0:T(8,128)(2,1)S(1)} copy(bf16[4,32,2,4096]{3,2,1,0:T(2,128)(2,1)} %param.14) | data formatting | bytes 4194304 | tf_op args[6]
  3.7 0.0 copy-done
  3.7 0.0 copy-done.1
  3.7 0.0 copy-done.2
  3.7 0.0 copy-done.3
  3.7 0.0 copy-done.4
  3.7 127.9 %shard_map.111 = (bf16[64,1024]{1,0:T(8,128)(2,1)S(1)}, bf16[64,1024]{1,0:T(8,128)(2,1)S(1)}, bf16[4,2,32,4096]{3,2,1,0:T(8,128)(2,1)S(1)}, f32[1,1024]{1,0:T(1,128)S(1)}) custom-call(s32[2,1,2]{2,1,0:T(1,128)S(1)} %copy-done.4, bf16[64,1024]{1,0:T(8,128)(2,1)S(1)} %bitcast.15, bf16[64,1024]{1,0:T(8,128)(2,1)S(1)} %bitcast.16, ...), custom_call_target="tpu_custom_call" | custom-call | flops 5000000000 | bytes 14680064 | tf_op jit(solution)/shard_map/pallas_call | solution.py:453
  131.6 3.5 %copy.13 = bf16[4,32,2,4096]{3,2,1,0:T(2,128)(2,1)} copy(bf16[4,32,2,4096]{3,1,2,0:T(8,128)(2,1)S(1)} %bitcast.11) | data formatting | bytes 4194304
  135.2 0.7 copy.19
  135.8 0.7 copy.20
  136.5 0.6 copy.21
Async XLA Ops:
  0.6 3.0 %copy-start = (bf16[1,64,1024]{2,1,0:T(8,128)(2,1)S(1)}, bf16[1,64,1024]{2,1,0:T(8,128)(2,1)}, u32[]{:S(2)}) copy-start(bf16[1,64,1024]{2,1,0:T(8,128)(2,1)} %param.8) | copy-start | bytes 393220
  0.6 3.0 %copy-start.1 = (bf16[1,64,1024]{2,1,0:T(8,128)(2,1)S(1)}, bf16[1,64,1024]{2,1,0:T(8,128)(2,1)}, u32[]{:S(2)}) copy-start(bf16[1,64,1024]{2,1,0:T(8,128)(2,1)} %param.9) | copy-start | bytes 393220
  0.7 3.0 %copy-start.2 = (bf16[1,64,1024]{2,1,0:T(8,128)(2,1)S(1)}, bf16[1,64,1024]{2,1,0:T(8,128)(2,1)}, u32[]{:S(2)}) copy-start(bf16[1,64,1024]{2,1,0:T(8,128)(2,1)} %param.10) | copy-start | bytes 393220
  0.7 3.0 %copy-start.3 = (f32[1,4096]{1,0:T(1,128)S(1)}, f32[1,4096]{1,0:T(1,128)}, u32[]{:S(2)}) copy-start(f32[1,4096]{1,0:T(1,128)} %gain_ref.1) | copy-start | bytes 49156
  0.7 3.0 %copy-start.4 = (s32[2,1,2]{2,1,0:T(1,128)S(1)}, s32[2,1,2]{2,1,0:T(1,128)}, u32[]{:S(2)}) copy-start(s32[2,1,2]{2,1,0:T(1,128)} %pat_ref.1) | copy-start | bytes 52
